TPU v7x, 512 devices: a whole 4x8x8 slice. The times are simulated.
512 devices in a mesh: section: 16 (over z, core), tensor: 32 (over y, x).
Axes of the slice: x: 4, y: 8, z: 8, core: 2. Of those that a mesh axis runs over, the one named last changes fastest.
Arguments:
- resid: bfloat16 [128, 3584], P('tensor'), may hold values from -6 to 6
- w_enc: bfloat16 [114688, 3584], P(('section', 'tensor')), may hold values from -0.09375 to 0.09375
- b_enc: float32 [114688], P(('section', 'tensor')), may hold values from -1 to 0.5
- w_dec: bfloat16 [114688, 3584], P(('section', 'tensor')), may hold values from -0.015625 to 0.015625
- b_dec: float32 [3584], replicated, may hold values from -3 to 3
Outputs:
- recon: float32 [128, 3584], P('tensor')
- grad_w_dec: bfloat16 [114688, 3584], P(('section', 'tensor'))
- code_grad: float32 [128, 114688], P(None, ('section', 'tensor'))
- grad_b_dec: float32 [3584], replicated
- loss_value: float32 [], replicated
All inputs are finite; a program needn't handle non-finite values.
Results may differ from a plain program's by a relative error of at most 0.0032.
The roundings to bfloat16 on the way count: a program that leaves them out, or rounds other values in their place, can miss the bound.
Values may be sent and summed in bfloat16 or wider, within the bound.
A program may use at most 64 MiB of HBM per device.

v0:
```python
import jax
import jax.numpy as jnp
from jax import lax
from jax.sharding import PartitionSpec as P

epsilon = 1e-06


def per_device(resid, w_enc, b_enc, w_dec, b_dec):
    stream = lax.all_gather(resid, "tensor", axis=0, tiled=True)
    preact = (
        lax.dot_general(stream, w_enc, (((1,), (1,)), ((), ())), preferred_element_type=jnp.float32)
        + b_enc
    )
    codes = jnp.maximum(preact, 0.0).astype(jnp.bfloat16)
    codes_f32 = codes.astype(jnp.float32)
    dec_f32 = w_dec.astype(jnp.float32)
    dec_norm = jnp.sqrt(jnp.sum(dec_f32 * dec_f32, axis=1) + epsilon)
    penalty = lax.psum(jnp.sum(codes_f32 * dec_norm), ("section", "tensor"))
    own_rows = resid.shape[0]
    total_rows = stream.shape[0]
    model_width = stream.shape[1]
    partial_value = jnp.dot(codes, w_dec, preferred_element_type=jnp.float32)
    summed = lax.psum(partial_value, ("section", "tensor"))
    recon_all = summed + b_dec
    errors = recon_all - stream.astype(jnp.float32)
    first_row = lax.axis_index("tensor") * own_rows
    recon = lax.dynamic_slice_in_dim(recon_all, first_row, own_rows, 0)
    squares = jnp.sum(errors * errors)
    grad_b_dec = jnp.sum(errors, axis=0)
    err_half = errors.astype(jnp.bfloat16)
    loss_value = (0.5 * squares + penalty) / (total_rows * model_width)
    code_sums = jnp.sum(codes_f32, axis=0)
    grad_w_dec = lax.dot_general(
        codes, err_half, (((0,), (0,)), ((), ())), preferred_element_type=jnp.float32
    )
    grad_w_dec = grad_w_dec + code_sums[:, None] * dec_f32 / dec_norm[:, None]
    code_grad = (
        lax.dot_general(
            err_half, w_dec, (((1,), (1,)), ((), ())), preferred_element_type=jnp.float32
        )
        + dec_norm
    )
    return (recon, grad_w_dec.astype(jnp.bfloat16), code_grad, grad_b_dec, loss_value)


def solution(mesh):
    in_specs = (
        P("tensor", None),
        P(("section", "tensor"), None),
        P(("section", "tensor")),
        P(("section", "tensor"), None),
        P(),
    )
    out_specs = (
        P("tensor", None),
        P(("section", "tensor"), None),
        P(None, ("section", "tensor")),
        P(),
        P(),
    )
    return jax.shard_map(
        per_device, mesh=mesh, in_specs=in_specs, out_specs=out_specs, check_vma=False
    )
```

profile of v0, /device:TPU:1, one launch (start us, length us, event | category | flops | bytes accessed | tf_op | source)
XLA Modules:
  0.0 361.0 jit_solution(16243876525081524570)
XLA Ops:
  7.2 0.0 copy-start
  7.2 0.0 all-reduce.2.cloned.1.call-start
  7.2 40.3 %all-gather = bf16[32,4,3584]{2,1,0:T(4,128)(2,1)S(1)} all-gather(bf16[1,4,3584]{2,1,0:T(4,128)(2,1)} %bitcast.7), channel_id=1, replica_groups=mesh['section'=16,'tensor'=32] {'tensor'}, dimensions={0}, use_global_device_ids=true | all-gather | bytes 946176 | tf_op jit(solution)/shard_map/all_gather | solution.py:10
  47.5 0.0 copy-start.4
  47.5 0.2 reshape.22
  47.7 0.0 copy-start.1
  47.7 1.9 fusion.2
  49.7 0.0 copy-done
  49.7 0.0 copy-done.4
  49.7 1.2 fusion.7
  50.9 0.0 copy-done.1
  50.9 0.0 copy-start.3
  50.9 1.7 fusion.10
  52.6 0.0 all-reduce.2.cloned.1.call-update
  52.6 114.0 %psum.15 = f32[]{:T(128)} all-reduce(f32[]{:T(128)} %get-tuple-element.7), channel_id=1, replica_groups=mesh['section'=16,'tensor'=32] {'section','tensor'}, use_global_device_ids=true, to_apply=%region_6.0 | all-reduce | flops 1 | bytes 8 | tf_op jit(solution)/shard_map/psum | solution.py:19
  166.6 178.5 %all-reduce.2.cloned.1.call-done = f32[128,3584]{1,0:T(8,128)} async-done(((f32[128,3584]{1,0:T(8,128)}), f32[128,3584]{1,0:T(8,128)}) %all-reduce.2.cloned.1.call-update) | async-done | bytes 1835024 | tf_op jit(solution)/shard_map/psum | solution.py:24
  345.2 0.0 copy-done.3
  345.2 0.0 copy-start.2
  345.2 2.8 multiply_reduce_fusion
  348.0 0.0 copy-done.2
  348.0 1.3 convolution_add_fusion.1
  349.3 1.9 fusion
  351.2 0.6 constant_dynamic-slice_fusion
  (1 shorter events, 0.0 us)
Async XLA Ops:
  7.2 42.5 %copy-start = (bf16[224,3584]{1,0:T(8,128)(2,1)S(1)}, bf16[224,3584]{1,0:T(8,128)(2,1)}, u32[]{:S(2)}) copy-start(bf16[224,3584]{1,0:T(8,128)(2,1)} %param.6) | copy-start | bytes 4816900
  7.2 338.0 %all-reduce.2.cloned.1.call-start = ((), (), s32[]{:S(2)}) async-start(), calls=%async_computation | async-start | bytes 3670016 | tf_op jit(solution)/shard_map/psum | solution.py:24
  47.5 2.2 copy-start.4
  47.7 3.2 copy-start.1
  50.9 294.3 %copy-start.3 = (f32[3584]{0:T(1024)S(1)}, f32[3584]{0:T(1024)}, u32[]{:S(2)}) copy-start(f32[3584]{0:T(1024)} %param.9) | copy-start | bytes 43012
  345.2 2.8 copy-start.2
Sparse Core Ops, SparseCore 0:
  52.7 292.4 all-reduce.1
where the time goes:
time: 361 us
  waiting for transfers between devices  179 us (50%)
  blocking collectives  154 us (43%)
  between operations  16.4 us (5%)
  matrix products  6.08 us (2%)
  other arithmetic  4.75 us (1%)
    psum x1, waiting for transfers between devices, per_device(): summed = lax.psum(partial_value, ('section', 'tensor'))  179 us
    psum x1, blocking collectives, per_device(): penalty = lax.psum(jnp.sum(codes_f32 * dec_norm), ('section', 'tensor'))  114 us
    all_gather x1, blocking collectives, per_device(): stream = lax.all_gather(resid, 'tensor', axis=0, tiled=True)  40.3 us
  transfers between devices with their start and end apart: 1, of which 1 were waited for; matrix products, arithmetic and copies ran while one was open for 0% of the time, Pallas kernels for 0%

commit v1 on v0

--- a/solution.py
+++ b/solution.py
@@ -7,7 +7,10 @@
 
 
 def per_device(resid, w_enc, b_enc, w_dec, b_dec):
-    stream = lax.all_gather(resid, "tensor", axis=0, tiled=True)
+    count = lax.axis_size("tensor")
+    blocks = jnp.stack([resid for _ in range(count)])
+    blocks = lax.all_to_all(blocks, "tensor", split_axis=0, concat_axis=0)
+    stream = jnp.concatenate(blocks, axis=0)
     preact = (
         lax.dot_general(stream, w_enc, (((1,), (1,)), ((), ())), preferred_element_type=jnp.float32)
         + b_enc

time: 361 us -> 346 us (0.958)
  blocking collectives: 154 us -> 106 us
  waiting for transfers between devices: 179 us -> 199 us
  starting transfers between devices: 0.04 us -> 10.7 us
  local copies, waits for them, and re-layouts: 0.87 us -> 4.59 us
    all_gather x1 -> x0, blocking collectives: 40.3 us -> none  [per_device(): stream = lax.all_gather(resid, 'tensor', axis=0, tiled=True)]
    all_to_all x0 -> x1, waiting for transfers between devices: none -> 23 us  [per_device(): blocks = lax.all_to_all(blocks, 'tensor', split_axis=0, concat_axis=0)]
    all_to_all x0 -> x1, starting transfers between devices: none -> 10.6 us  [per_device(): blocks = lax.all_to_all(blocks, 'tensor', split_axis=0, concat_axis=0)]
    psum x1, blocking collectives: 114 us -> 106 us  [per_device(): penalty = lax.psum(jnp.sum(codes_f32 * dec_norm), ('section', 'tensor'))]
  transfers between devices with their start and end apart: 1 -> 2, of which waited for: 1 -> 2; matrix products, arithmetic and copies ran while one was open for 0% -> 0% of each run, Pallas kernels for 0% -> 0%
where the time goes in v1:
time: 346 us
  waiting for transfers between devices  199 us (58%)
  blocking collectives  106 us (31%)
  between operations  16.4 us (5%)
  starting transfers between devices  10.7 us (3%)
  matrix products  6.08 us (2%)
  local copies, waits for them, and re-layouts  4.59 us (1%)
    psum x1, waiting for transfers between devices, per_device(): summed = lax.psum(partial_value, ('section', 'tensor'))  176 us
    psum x1, blocking collectives, per_device(): penalty = lax.psum(jnp.sum(codes_f32 * dec_norm), ('section', 'tensor'))  106 us
    all_to_all x1, waiting for transfers between devices, per_device(): blocks = lax.all_to_all(blocks, 'tensor', split_axis=0, concat_axis=0)  23 us
    all_to_all x1, starting transfers between devices, per_device(): blocks = lax.all_to_all(blocks, 'tensor', split_axis=0, concat_axis=0)  10.6 us
  transfers between devices with their start and end apart: 2, of which 2 were waited for; matrix products, arithmetic and copies ran while one was open for 0% of the time, Pallas kernels for 0%

profile of v1, /device:TPU:1, one launch (start us, length us, event | category | flops | bytes accessed | tf_op | source)
XLA Modules:
  0.0 346.0 jit_solution(4959216329781461694)
XLA Ops:
  7.2 0.0 copy-start
  7.2 0.0 copy-start.1
  7.2 2.1 stack.2
  9.3 10.6 %all-to-all-start = ((bf16[32,4,3584]{2,1,0:T(4,128)(2,1)}), bf16[32,4,3584]{2,1,0:T(4,128)(2,1)}, u32[]{:S(2)}, u32[]{:S(2)}) async-start(bf16[32,4,3584]{2,1,0:T(4,128)(2,1)} %stack.2), calls=%async_computation | async-start | bytes 1835008 | tf_op jit(solution)/shard_map/all_to_all | solution.py:12
  19.9 0.0 copy-start.5
  19.9 0.0 all-reduce.2.cloned.1.call-start
  19.9 0.0 copy-done.1
  19.9 0.4 fusion.2
  20.4 23.0 %all-to-all-done = bf16[32,4,3584]{2,1,0:T(4,128)(2,1)} async-done(((bf16[32,4,3584]{2,1,0:T(4,128)(2,1)}), bf16[32,4,3584]{2,1,0:T(4,128)(2,1)}, u32[]{:S(2)}, u32[]{:S(2)}) %all-to-all-start) | async-done | bytes 917536 | tf_op jit(solution)/shard_map/all_to_all | solution.py:12
  43.3 1.7 reshape.26
  45.0 0.0 copy-done
  45.0 0.0 copy-done.5
  45.0 0.0 copy-start.2
  45.0 1.2 fusion.7
  46.2 0.2 copy-done.2
  46.4 1.7 fusion.10
  48.1 0.0 all-reduce.2.cloned.1.call-update
  48.1 106.0 %psum.15 = f32[]{:T(128)} all-reduce(f32[]{:T(128)} %get-tuple-element.7), channel_id=1, replica_groups=mesh['section'=16,'tensor'=32] {'section','tensor'}, use_global_device_ids=true, to_apply=%region_6.0 | all-reduce | flops 1 | bytes 8 | tf_op jit(solution)/shard_map/psum | solution.py:22
  154.1 176.1 %all-reduce.2.cloned.1.call-done = f32[128,3584]{1,0:T(8,128)} async-done(((f32[128,3584]{1,0:T(8,128)}), f32[128,3584]{1,0:T(8,128)}) %all-reduce.2.cloned.1.call-update) | async-done | bytes 1835024 | tf_op jit(solution)/shard_map/psum | solution.py:27
  330.2 0.0 copy-done.4
  330.2 2.8 multiply_reduce_fusion
  333.0 1.3 convolution_add_fusion.1
  334.3 1.9 fusion
  336.2 0.6 constant_dynamic-slice_fusion
  (4 shorter events, 0.0 us)
Async XLA Ops:
  7.2 37.8 %copy-start = (bf16[224,3584]{1,0:T(8,128)(2,1)S(1)}, bf16[224,3584]{1,0:T(8,128)(2,1)}, u32[]{:S(2)}) copy-start(bf16[224,3584]{1,0:T(8,128)(2,1)} %param.6) | copy-start | bytes 4816900
  7.2 12.8 %copy-start.1 = (bf16[224,3584]{1,0:T(8,128)(2,1)S(1)}, bf16[224,3584]{1,0:T(8,128)(2,1)}, u32[]{:S(2)}) copy-start(bf16[224,3584]{1,0:T(8,128)(2,1)} %param.8) | copy-start | bytes 4816900
  9.3 34.1 %all-to-all-start = ((bf16[32,4,3584]{2,1,0:T(4,128)(2,1)}), bf16[32,4,3584]{2,1,0:T(4,128)(2,1)}, u32[]{:S(2)}, u32[]{:S(2)}) async-start(bf16[32,4,3584]{2,1,0:T(4,128)(2,1)} %stack.2), calls=%async_computation | async-start | bytes 1835008 | tf_op jit(solution)/shard_map/all_to_all | solution.py:12
  19.9 25.1 %copy-start.5 = (f32[224]{0:T(256)S(1)}, f32[224]{0:T(256)}, u32[]{:S(2)}) copy-start(f32[224]{0:T(256)} %param.7) | copy-start | bytes 2692
  19.9 310.3 %all-reduce.2.cloned.1.call-start = ((), (), s32[]{:S(2)}) async-start(), calls=%async_computation.1 | async-start | bytes 3670016 | tf_op jit(solution)/shard_map/psum | solution.py:27
  45.0 1.4 copy-start.2
  46.4 283.8 %copy-start.4 = (f32[3584]{0:T(1024)S(1)}, f32[3584]{0:T(1024)}, u32[]{:S(2)}) copy-start(f32[3584]{0:T(1024)} %param.9) | copy-start | bytes 43012
  330.2 2.8 copy-start.3
Sparse Core Ops, SparseCore 0:
  48.2 281.8 all-reduce.1
